TPU v7x, 128 devices: a whole 4x4x4 slice. The times are simulated.
128 devices in a mesh: row: 4 (over y_lo, core), col: 32 (over y_hi, x, z).
Axes of the slice: x: 4, y: 4 (y_hi: 2, y_lo: 2; y = y_hi * 2 + y_lo), z: 4, core: 2. Of those that a mesh axis runs over, the one named last changes fastest.
Arguments:
- fringes: bfloat16 [32768, 32768], P(('row', 'col')), may hold values from -24 to 24
- lobe_bounds: int32 [64, 2], replicated, may hold values from 0 to 4096, as said below
- zone_index: int32 [1024, 64], P(('row', 'col')), may hold values from 0 to 4095
- zone_table: float32 [4, 4096], P(None, ('row', 'col')), may hold values from -6 to 6
Outputs:
- heights: bfloat16 [16384, 32768], P(('row', 'col'))
Inputs may be any that keep to these rules, and one draw needn't show every extreme that they name: For every band t, lobe_bounds[t, 0] < lobe_bounds[t, 1]; some band starts at 0 and some band ends at 4096.
All inputs are finite; a program needn't handle non-finite values.
Results may differ from a plain program's by a relative error of at most 0.023.
Values may be sent and summed in bfloat16 or wider, within the bound.
A program may use at most 128 MiB of HBM per device.

v0:
```python
import math

import jax
import jax.numpy as jnp
from jax import lax
from jax.sharding import PartitionSpec as P

W = 32768
H = 32768
W1 = 128
H1 = 128
KY_TILES = 64
ZB_R = 16
ZB_C = 512
LOBE = 4096
LOBE_START = 4096


damping_floor = 0.5


def phase_pair(first_count, second_count, period, offset):
    first_index = jnp.arange(first_count, dtype=jnp.int32)[:, None]
    second_index = jnp.arange(second_count, dtype=jnp.int32)[None, :] + offset
    turn_count = first_index * second_index % period
    angles = turn_count.astype(jnp.float32) * (2.0 * math.pi / period)
    return (jnp.cos(angles), jnp.sin(angles))


def table_pair(first_count, second_count, period, offset):
    cosine, sine_part = phase_pair(first_count, second_count, period, offset)
    return (cosine.astype(jnp.bfloat16), sine_part.astype(jnp.bfloat16))


def complex_mix(pattern, real_part, imag_part, cosine, sine_part, direction):
    real_cos = jnp.einsum(pattern, real_part, cosine, preferred_element_type=jnp.float32)
    imag_sin = jnp.einsum(pattern, imag_part, sine_part, preferred_element_type=jnp.float32)
    imag_cos = jnp.einsum(pattern, imag_part, cosine, preferred_element_type=jnp.float32)
    real_sin = jnp.einsum(pattern, real_part, sine_part, preferred_element_type=jnp.float32)
    return (real_cos - direction * imag_sin, imag_cos + direction * real_sin)


def apply_twist(real_part, imag_part, cosine, sine_part, direction):
    out_real = real_part * cosine - direction * (imag_part * sine_part)
    out_imag = imag_part * cosine + direction * (real_part * sine_part)
    return (out_real, out_imag)


def row_forward(rows_block):
    row_total = rows_block.shape[0]
    shaped = rows_block.reshape(row_total, W1, W // W1)
    cosine, sine_part = table_pair(W1, W1, W1, 0)
    first_real = jnp.einsum("rab,ak->rkb", shaped, cosine, preferred_element_type=jnp.float32)
    first_imag = -jnp.einsum("rab,ak->rkb", shaped, sine_part, preferred_element_type=jnp.float32)
    twist_real, twist_imag = phase_pair(W1, W // W1, W, 0)
    middle_real, middle_imag = apply_twist(first_real, first_imag, twist_real, twist_imag, -1.0)
    middle_real = middle_real.astype(jnp.bfloat16)
    middle_imag = middle_imag.astype(jnp.bfloat16)
    cosine, sine_part = table_pair(W // W1, LOBE // W1, W // W1, LOBE_START // W1)
    lobe_real, lobe_imag = complex_mix(
        "rkb,bj->jkr", middle_real, middle_imag, cosine, sine_part, -1.0
    )
    return jnp.stack([lobe_real, lobe_imag]).reshape(2, LOBE, row_total).astype(jnp.bfloat16)


def column_pass(columns, column_index, lower_edge, upper_edge):
    col_total = columns.shape[1]
    second_len = H // H1
    shaped_real = columns[0].reshape(col_total, H1, second_len)
    shaped_imag = columns[1].reshape(col_total, H1, second_len)
    cosine, sine_part = table_pair(H1, H1, H1, 0)
    first_real, first_imag = complex_mix(
        "cab,ak->ckb", shaped_real, shaped_imag, cosine, sine_part, -1.0
    )
    twist_real, twist_imag = phase_pair(H1, second_len, H, 0)
    middle_real, middle_imag = apply_twist(first_real, first_imag, twist_real, twist_imag, -1.0)
    middle_real = middle_real.astype(jnp.bfloat16)
    middle_imag = middle_imag.astype(jnp.bfloat16)
    cosine, sine_part = table_pair(second_len, second_len, second_len, 0)
    spectrum_real, spectrum_imag = complex_mix(
        "ckb,bm->cmk", middle_real, middle_imag, cosine, sine_part, -1.0
    )
    spectrum_real = spectrum_real.reshape(col_total, H)
    spectrum_imag = spectrum_imag.reshape(col_total, H)
    lower_rows = jnp.repeat(lower_edge, H // KY_TILES)
    upper_rows = jnp.repeat(upper_edge, H // KY_TILES)
    keep_mask = (column_index[:, None] >= lower_rows[None, :]) & (
        column_index[:, None] < upper_rows[None, :]
    )
    masked_real = jnp.where(keep_mask, spectrum_real, 0.0)
    masked_imag = jnp.where(keep_mask, spectrum_imag, 0.0)
    half_rows = H // 2
    fold_scale = 1.0 / (H * W)
    folded_real = ((masked_real[:, :half_rows] + masked_real[:, half_rows:]) * fold_scale).astype(
        jnp.bfloat16
    )
    folded_imag = ((masked_imag[:, :half_rows] + masked_imag[:, half_rows:]) * fold_scale).astype(
        jnp.bfloat16
    )
    fold_len = second_len // 2
    folded_real = folded_real.reshape(col_total, fold_len, H1)
    folded_imag = folded_imag.reshape(col_total, fold_len, H1)
    cosine, sine_part = table_pair(fold_len, fold_len, fold_len, 0)
    half_real, half_imag = complex_mix(
        "cmk,mq->cqk", folded_real, folded_imag, cosine, sine_part, 1.0
    )
    twist_real, twist_imag = phase_pair(fold_len, H1, half_rows, 0)
    middle_real, middle_imag = apply_twist(half_real, half_imag, twist_real, twist_imag, 1.0)
    middle_real = middle_real.astype(jnp.bfloat16)
    middle_imag = middle_imag.astype(jnp.bfloat16)
    cosine, sine_part = table_pair(H1, H1, H1, 0)
    out_real, out_imag = complex_mix(
        "cqk,kp->cpq", middle_real, middle_imag, cosine, sine_part, 1.0
    )
    return jnp.stack([out_real, out_imag]).reshape(2, col_total, half_rows).astype(jnp.bfloat16)


def height_map(field_real, field_imag, coefficients):
    magnitude = jnp.sqrt(field_real * field_real + field_imag * field_imag)
    sine_value = field_imag / jnp.maximum(magnitude, damping_floor)
    row_total = field_real.shape[0]
    sine_value = sine_value.reshape(row_total // ZB_R, ZB_R, W // ZB_C, ZB_C)
    expanded = coefficients[:, :, None, :, None]
    heights = expanded[0] + sine_value * (
        expanded[1] + sine_value * (expanded[2] + sine_value * expanded[3])
    )
    return heights.reshape(row_total, W).astype(jnp.bfloat16)


def row_inverse(segment, coefficients):
    row_total = segment.shape[2]
    shaped_real = segment[0].reshape(LOBE // W1, W1, row_total)
    shaped_imag = segment[1].reshape(LOBE // W1, W1, row_total)
    cosine, sine_part = table_pair(LOBE // W1, W // W1, W // W1, 0)
    pixel_real, pixel_imag = complex_mix(
        "jkr,jq->rkq", shaped_real, shaped_imag, cosine, sine_part, 1.0
    )
    twist_real, twist_imag = phase_pair(W1, W // W1, W, 0)
    middle_real, middle_imag = apply_twist(pixel_real, pixel_imag, twist_real, twist_imag, 1.0)
    middle_real = middle_real.astype(jnp.bfloat16)
    middle_imag = middle_imag.astype(jnp.bfloat16)
    cosine, sine_part = table_pair(W1, W1, W1, 0)
    field_real, field_imag = complex_mix(
        "rkq,kp->rpq", middle_real, middle_imag, cosine, sine_part, 1.0
    )
    return height_map(
        field_real.reshape(row_total, W), field_imag.reshape(row_total, W), coefficients
    )


def body(fringes, lobe_bounds, zone_index, zone_table):
    row_count = fringes.shape[0]
    row_block = math.gcd(row_count, 64)

    def fill_block(block_number, buffer):
        row_start = block_number * row_block
        rows_block = lax.dynamic_slice_in_dim(fringes, row_start, row_block, 0)
        return lax.dynamic_update_slice_in_dim(buffer, row_forward(rows_block), row_start, 2)

    stacked = lax.fori_loop(
        0, row_count // row_block, fill_block, jnp.zeros((2, LOBE, row_count), jnp.bfloat16)
    )
    row_size = lax.axis_size("row")
    col_size = lax.axis_size("col")
    local_cols = LOBE // (row_size * col_size)
    columns = lax.all_to_all(stacked, ("row", "col"), split_axis=1, concat_axis=2, tiled=True)
    column_index = lax.axis_index(("row", "col")) * local_cols + jnp.arange(
        local_cols, dtype=jnp.int32
    )
    field_cols = column_pass(columns, column_index, lobe_bounds[:, 0], lobe_bounds[:, 1])
    out_count = field_cols.shape[2] // (row_size * col_size)
    field_rows = lax.all_to_all(field_cols, ("row", "col"), split_axis=2, concat_axis=1, tiled=True)
    full_table = lax.all_gather(zone_table, ("row", "col"), axis=1, tiled=True)
    zone_count = full_table.shape[1]
    flat_zones = zone_index.reshape(-1)
    onehot = (jnp.arange(zone_count, dtype=jnp.int32)[:, None] == flat_zones[None, :]).astype(
        jnp.float32
    )
    coefficients = jnp.dot(
        full_table, onehot, precision=lax.Precision.HIGHEST, preferred_element_type=jnp.float32
    )
    coefficients = coefficients.reshape(4, zone_index.shape[0], zone_index.shape[1])

    def height_block(block_number, buffer):
        row_start = block_number * ZB_R
        segment = lax.dynamic_slice_in_dim(field_rows, row_start, ZB_R, 2)
        block_coefficients = lax.dynamic_slice_in_dim(coefficients, block_number, 1, 1)
        return lax.dynamic_update_slice_in_dim(
            buffer, row_inverse(segment, block_coefficients), row_start, 0
        )

    return lax.fori_loop(
        0, out_count // ZB_R, height_block, jnp.zeros((out_count, W), jnp.bfloat16)
    )


def solution(mesh):
    placed = (P(("row", "col"), None), P(), P(("row", "col"), None), P(None, ("row", "col")))
    return jax.shard_map(
        body, mesh=mesh, in_specs=placed, out_specs=P(("row", "col"), None), check_vma=False
    )
```

profile of v0, /device:TPU:16, one launch (start us, length us, event | category | flops | bytes accessed | tf_op | source)
XLA Modules:
  0.0 755.8 jit_solution(3640786369073632010)
XLA Ops:
  2.5 83.2 %while.32 = (s32[]{:T(128)}, bf16[2,4096,256]{1,2,0:T(8,128)(2,1)}, bf16[256,32768]{1,0:T(8,128)(2,1)}, s32[]{:T(128)}, s32[]{:T(128)}, /*index=5*/s32[]{:T(128)}, s32[]{:T(128)}) while((s32[]{:T(128)}, bf16[2,4096,256]{1,2,0:T(8,128)(2,1)}, bf16[256,32768]{1,0:T(8,128)(2,1)}, s32[]{:T(128)}, s32[]{:T(128)}, /*index=5*/s32[]{:T(128)}, ...), condition=%wide.region_1.2_spmd, body=%wide.region_0.1_spmd.sunk | while | flops 1638793216 | bytes 127402848 | solution.py:160
  8.1 3.9 fusion.362
  16.9 3.7 convolution_multiply_fusion.4
  28.9 3.9 fusion.362
  37.7 3.7 convolution_multiply_fusion.4
  49.7 3.9 fusion.362
  58.5 3.7 convolution_multiply_fusion.4
  70.5 3.9 fusion.362
  79.3 3.7 convolution_multiply_fusion.4
  85.7 11.2 %copy.53 = bf16[2,4096,256]{2,0,1:T(2,128)(2,1)} copy(bf16[2,4096,256]{1,2,0:T(8,128)(2,1)} %get-tuple-element.249) | data formatting | bytes 8388608 | tf_op jit(solution)/shard_map/while | solution.py:160
  96.9 11.1 %all-to-all-start = ((bf16[2,4096,256]{2,0,1:T(2,128)(2,1)}), bf16[2,4096,256]{2,0,1:T(2,128)(2,1)}, u32[]{:S(2)}, u32[]{:S(2)}) async-start(bf16[2,4096,256]{2,0,1:T(2,128)(2,1)} %copy.53), calls=%async_computation | async-start | bytes 8388608 | tf_op jit(solution)/shard_map/all_to_all | solution.py:166
  109.5 49.3 %all-to-all-done = bf16[2,4096,256]{2,0,1:T(2,128)(2,1)} async-done(((bf16[2,4096,256]{2,0,1:T(2,128)(2,1)}), bf16[2,4096,256]{2,0,1:T(2,128)(2,1)}, u32[]{:S(2)}, u32[]{:S(2)}) %all-to-all-start) | async-done | bytes 4194336 | tf_op jit(solution)/shard_map/all_to_all | solution.py:166
  158.9 4.6 copy.88
  166.2 2.7 fusion.144
  175.5 6.5 bitcast_select_fusion
  196.6 12.8 %copy.58 = bf16[2,32,16384]{1,0,2:T(2,128)(2,1)} copy(bf16[2,32,16384]{2,1,0:T(8,128)(2,1)S(1)} %pad_maximum_fusion) | data formatting | bytes 4194304 | tf_op jit(solution)/shard_map/stack | solution.py:115
  209.4 17.9 %reshape.361 = bf16[128,2,4096]{2,1,0:T(2,128)(2,1)} reshape(bf16[16384,2,32]{2,1,0:T(2,128)(2,1)} %bitcast.332) | data formatting | bytes 4194304
  227.3 9.1 %all-to-all-start.1 = ((bf16[128,2,4096]{2,1,0:T(2,128)(2,1)}), bf16[128,2,4096]{2,1,0:T(2,128)(2,1)S(1)}, u32[]{:S(2)}, u32[]{:S(2)}) async-start(bf16[128,2,4096]{2,1,0:T(2,128)(2,1)} %reshape.361), calls=%async_computation.1 | async-start | bytes 4194304 | tf_op jit(solution)/shard_map/all_to_all | solution.py:172
  236.4 368.7 %all-gather = f32[128,32,4]{1,2,0:T(4,128)S(1)} all-gather(f32[1,32,4]{1,2,0:T(4,128)S(1)} %bitcast.351), channel_id=1, replica_groups=mesh['row'=4,'col'=32] {'row','col'}, dimensions={0}, use_global_device_ids=true | all-gather | bytes 66048 | tf_op jit(solution)/shard_map/all_gather | solution.py:173
  607.9 6.4 reshape.362
  614.3 15.8 %copy.69 = bf16[2,32,128,128]{3,1,2,0:T(8,128)(2,1)S(1)} copy(bf16[2,32,128,128]{1,0,3,2:T(2,128)(2,1)} %bitcast.333) | data formatting | bytes 4194304 | tf_op jit(solution)/shard_map/all_to_all | solution.py:172
  630.2 2.8 copy.61
  633.0 4.2 broadcast_in_dim.51
  637.2 118.4 %while.33 = (s32[]{:T(128)}, bf16[128,32768]{1,0:T(8,128)(2,1)}, f32[4,8,64]{2,1,0:T(8,128)S(1)}, bf16[2,4096,128]{1,2,0:T(8,128)(2,1)}, s32[]{:T(128)}, /*index...) while((s32[]{:T(128)}, bf16[128,32768]{1,0:T(8,128)(2,1)}, f32[4,8,64]{2,1,0:T(8,128)S(1)}, ...), condition=%wide.region_3.4_spmd, body=%wide.region_2.3_spmd.sunk | while | flops 685604864 | bytes 49286364 | solution.py:192
  648.2 3.8 fusion.387
  663.0 3.8 fusion.387
  677.8 3.8 fusion.387
  692.6 3.8 fusion.387
  707.4 3.8 fusion.387
  722.2 3.8 fusion.387
  737.0 3.8 fusion.387
  751.8 3.8 fusion.387
  (283 shorter events, 169.9 us)
Async XLA Ops:
  12.0 1.9 copy-start
  12.0 3.3 copy-start.2
  16.9 3.7 copy-start.1
  32.8 1.9 copy-start
  32.8 3.3 copy-start.2
  37.7 3.7 copy-start.1
  53.6 1.9 copy-start
  53.6 3.3 copy-start.2
  58.5 3.7 copy-start.1
  74.4 1.9 copy-start
  74.4 3.3 copy-start.2
  79.3 3.7 copy-start.1
  96.9 11.2 %copy-start.6 = (s32[64,2]{0,1:T(2,128)S(1)}, s32[64,2]{0,1:T(2,128)}, u32[]{:S(2)}) copy-start(s32[64,2]{0,1:T(2,128)} %param.9) | copy-start | bytes 1540
  96.9 61.9 %all-to-all-start = ((bf16[2,4096,256]{2,0,1:T(2,128)(2,1)}), bf16[2,4096,256]{2,0,1:T(2,128)(2,1)}, u32[]{:S(2)}, u32[]{:S(2)}) async-start(bf16[2,4096,256]{2,0,1:T(2,128)(2,1)} %copy.53), calls=%async_computation | async-start | bytes 8388608 | tf_op jit(solution)/shard_map/all_to_all | solution.py:166
  192.8 2.4 copy-start.3
  227.3 9.1 %copy-start.5 = (f32[4,32]{1,0:T(4,128)S(1)}, f32[4,32]{1,0:T(4,128)}, u32[]{:S(2)}) copy-start(f32[4,32]{1,0:T(4,128)} %param.11) | copy-start | bytes 1540
  227.3 378.0 %copy-start.4 = (s32[8,64]{1,0:T(8,128)S(1)}, s32[8,64]{1,0:T(8,128)}, u32[]{:S(2)}) copy-start(s32[8,64]{1,0:T(8,128)} %param.10) | copy-start | bytes 6148
  227.3 380.7 %all-to-all-start.1 = ((bf16[128,2,4096]{2,1,0:T(2,128)(2,1)}), bf16[128,2,4096]{2,1,0:T(2,128)(2,1)S(1)}, u32[]{:S(2)}, u32[]{:S(2)}) async-start(bf16[128,2,4096]{2,1,0:T(2,128)(2,1)} %reshape.361), calls=%async_computation.1 | async-start | bytes 4194304 | tf_op jit(solution)/shard_map/all_to_all | solution.py:172
where the time goes:
time: 764 us; the launch traced here: 756 us
  blocking collectives  369 us (48%)
  local copies, waits for them, and re-layouts  148 us (19%)
  matrix products  117 us (15%)
  other arithmetic  50.7 us (7%)
  waiting for transfers between devices  49.3 us (6%)
  starting transfers between devices  20.2 us (3%)
    all_gather x1, blocking collectives, body(): full_table = lax.all_gather(zone_table, ('row', 'col'), axis=1, tiled=True)  369 us
    while x116, local copies, waits for them, and re-layouts  52.5 us
    all_to_all x1, waiting for transfers between devices, body(): lax.all_to_all(stacked, ('row', 'col'), split_axis=1, concat_axis=2, tile...  49.3 us
    dynamic_update_slice x8, other arithmetic, height_block(): lax.dynamic_update_slice_in_dim(buffer, row_inverse(segment, block_coeffi...  30.6 us
    dot_general x24, matrix products, complex_mix(): jnp.einsum(pattern, real_part, sine_part, preferred_element_type=jnp.floa...  29.4 us
    dot_general x24, matrix products, complex_mix(): jnp.einsum(pattern, imag_part, sine_part, preferred_element_type=jnp.floa...  25.6 us
    unnamed x16, local copies, waits for them, and re-layouts  25.1 us
    dot_general x24, matrix products, complex_mix(): jnp.einsum(pattern, imag_part, cosine, preferred_element_type=jnp.float32)  18.9 us
  transfers between devices with their start and end apart: 2, of which 1 were waited for; matrix products, arithmetic and copies ran while one was open for 1% of the time, Pallas kernels for 0%

commit v1 on v0

v1 whole, which is shorter than its diff:
```python
import functools
import math

import jax
import jax.numpy as jnp
import ml_dtypes
import numpy as np
from jax import lax
from jax.experimental import pallas as pl
from jax.experimental.pallas import tpu as pltpu
from jax.sharding import PartitionSpec as P

W = 32768
H = 32768
LOBE = 4096
LOBE_START = 4096
DEVICES = 128
ROWS = H // DEVICES
HALF = ROWS // 2
KEPT = H // (2 * DEVICES)
GROUP = 32
ZB_R = 16

damping_floor = 0.5
bf16 = jnp.bfloat16
f32 = jnp.float32
MESH = pl.DeviceIdType.MESH


def turns(first, second, period):
    angles = (np.outer(first, second) % period).astype(np.float64) * (2.0 * math.pi / period)
    return np.cos(angles), np.sin(angles)


def make_tables():
    n4, n8, n16, n32 = (np.arange(n) for n in (4, 8, 16, 32))
    n128, n256, n1024, n2048 = (np.arange(n) for n in (128, 256, 1024, 2048))
    half = {}
    full = {}
    cosine, sine = turns(n16, n16, 16)
    half["row_a"] = np.kron(np.concatenate([cosine[:9], -sine[1:8]], 0), np.eye(16))
    cosine, sine = turns(n16, n2048, W)
    full["row_twist"] = np.broadcast_to(
        np.stack([cosine, sine], 1)[:, :, None, :], (16, 2, 8, 2048)
    )
    sides = []
    for odd in range(2):
        cosine, sine = turns(n1024, LOBE_START // 16 + 2 * n128 + odd, 2048)
        real = np.concatenate([cosine, sine], 0).reshape(2048, 4, 2, 16)
        imag = np.concatenate([-sine, cosine], 0).reshape(2048, 4, 2, 16)
        sides.append(np.stack([real, imag], 3).reshape(2048, 256))
    half["row_b"] = np.stack(sides)
    cosine, sine = turns(n128, n128, 128)
    half["col_a"] = np.block([[cosine, sine], [-sine, cosine]])
    half["col_m"] = np.block([[cosine, sine], [-sine, cosine]])
    half["col_p"] = np.block([[cosine, -sine], [sine, cosine]])
    cosine, sine = turns(n128, n256, H)
    full["col_twist"] = np.stack([cosine, sine])
    cosine, sine = turns(n256, n256, 256)
    half["col_b"] = np.block([[cosine, -sine], [sine, cosine]])
    cosine, sine = turns(n128, n128, H // 2)
    full["half_twist"] = np.stack([cosine, sine])
    cosine, sine = turns(n128, n1024, 1024)
    real = np.stack([cosine.reshape(128, 8, 128), sine.reshape(128, 8, 128)], 2).reshape(128, 2048)
    imag = np.stack([-sine.reshape(128, 8, 128), cosine.reshape(128, 8, 128)], 2).reshape(128, 2048)
    half["pix_j"] = np.stack([real.reshape(4, 2, 16, 2048), imag.reshape(4, 2, 16, 2048)], 2).reshape(
        256, 2048
    )
    cosine, sine = turns(n32, n1024, W)
    full["pix_twist"] = np.broadcast_to(
        np.stack([cosine, sine], 1)[:, :, None, :], (32, 2, 8, 1024)
    )
    mats = []
    for p0 in range(4):
        cosine, sine = turns(p0 + 4 * n8, n8, 32)
        block = np.stack(
            [np.stack([cosine, -sine], -1), np.stack([sine, cosine], -1)], 1
        ).reshape(16, 16)
        mats.append(np.kron(block, np.eye(16)))
    half["pix_k"] = np.stack(mats)
    made = {name: value.astype(ml_dtypes.bfloat16) for name, value in half.items()}
    made.update({name: np.ascontiguousarray(value, np.float32) for name, value in full.items()})
    return made


def dot(left, right):
    return jnp.dot(left, right, preferred_element_type=f32)


def at(start, size):
    return pl.ds(pl.multiple_of(start, size), size)


def row_first(block, tile, rows16, mat, twist, mid):
    sides = []
    for upper in range(2):
        sides.append(
            jnp.concatenate(
                [
                    block[pl.ds(rows16 * 16, 16), at(2048 * a + 1024 * upper + tile * 128, 128)]
                    for a in range(16)
                ],
                axis=0,
            )
        )
    mixed = dot(mat[...], jnp.concatenate(sides, axis=1))
    low = at(tile * 128, 128)
    high = at(1024 + tile * 128, 128)

    def part(index, upper):
        return mixed[index * 16 : (index + 1) * 16, upper * 128 : (upper + 1) * 128]

    def factor(k, index, place):
        value = twist[k, index, :, place]
        return jnp.concatenate([value, value], axis=0)

    for k in range(16):
        twisted = []
        for upper, place in ((0, low), (1, high)):
            source = k if k <= 8 else 16 - k
            real = part(source, upper)
            if k == 0:
                twisted.append((real, None))
                continue
            cosine = factor(k, 0, place)
            sine = factor(k, 1, place)
            if k == 8:
                twisted.append((real * cosine, -(real * sine)))
                continue
            imag = part(source + 8, upper)
            if k < 8:
                twisted.append((real * cosine + imag * sine, imag * cosine - real * sine))
            else:
                twisted.append((real * cosine - imag * sine, -(imag * cosine + real * sine)))
        (real0, imag0), (real1, imag1) = twisted
        rows = pl.ds(k * GROUP + rows16 * 16, 16)
        mid[0, rows, low] = (real0 + real1).astype(bf16)
        mid[1, rows, low] = (real0 - real1).astype(bf16)
        if imag0 is None:
            mid[0, rows, high] = jnp.zeros((16, 128), bf16)
            mid[1, rows, high] = jnp.zeros((16, 128), bf16)
        else:
            mid[0, rows, high] = (imag0 + imag1).astype(bf16)
            mid[1, rows, high] = (imag0 - imag1).astype(bf16)


def row_second(mid, odd, block, mat, lobe, group):
    rows = 8 * GROUP
    mixed = dot(mid[odd, at(block * rows, rows), :], mat[odd]).astype(bf16)
    for k in range(8):
        lobe[odd * 16 + block * 8 + k, at(group * GROUP, GROUP), :] = mixed[
            k * GROUP : (k + 1) * GROUP
        ]


def column_pair(pair, chunk, first_column, gather, mats, twists, edges, field):
    col_a, col_b, col_m, col_p = mats
    col_twist, half_twist = twists
    middles = []
    for u in range(2):
        j = pair * 2 + u
        parts = []
        for part in range(2):
            parts.append(
                jnp.concatenate(
                    [gather[h, pl.ds(part * 16 + j, DEVICES, stride=32), :] for h in range(2)],
                    axis=1,
                )
            )
        mixed = dot(col_a[...], jnp.concatenate(parts, axis=0).astype(bf16))
        real, imag = mixed[:128], mixed[128:]
        cosine, sine = col_twist[0], col_twist[1]
        middles.append(
            jnp.concatenate(
                [
                    (real * cosine + imag * sine).astype(bf16),
                    (imag * cosine - real * sine).astype(bf16),
                ],
                axis=1,
            )
        )
    spectrum = dot(jnp.concatenate(middles, axis=0), col_b[...])
    folded = []
    for u in range(2):
        column = first_column + 32 * (chunk * 16 + pair * 2 + u)
        keep = jnp.where((column >= edges[0:1, :]) & (column < edges[1:2, :]), 1.0 / (H * W), 0.0)
        rows = spectrum[u * 128 : (u + 1) * 128]
        folded.append(
            jnp.concatenate(
                [
                    (
                        rows[:, part * 256 : part * 256 + 128] * keep[:, :128]
                        + rows[:, part * 256 + 128 : part * 256 + 256] * keep[:, 128:]
                    ).astype(bf16)
                    for part in range(2)
                ],
                axis=1,
            )
        )
    halves = dot(jnp.concatenate(folded, axis=0), col_m[...])
    cosine, sine = half_twist[0], half_twist[1]
    terms = []
    for u in range(2):
        rows = halves[u * 128 : (u + 1) * 128]
        real, imag = rows[:, :128], rows[:, 128:]
        terms.append(
            jnp.concatenate(
                [
                    (real * cosine - imag * sine).astype(bf16),
                    (imag * cosine + real * sine).astype(bf16),
                ],
                axis=0,
            )
        )
    out = dot(col_p[...], jnp.concatenate(terms, axis=1))
    for u in range(2):
        field[at((pair * 2 + u) * 256, 256), :] = out[:, u * 128 : (u + 1) * 128]


def spectrum_kernel(
    fringes, edges, zones, row_a, row_twist, row_b, col_a, col_b, col_m, col_p, col_twist, half_twist,
    out, zones_out,
    block, mid, lobe, send_a, send_b, recv_a, recv_b, gather, field, send_c,
    load_sem, send_sem, recv_sem, own_sem,
):
    my_row = lax.axis_index("row")
    my_col = lax.axis_index("col")
    cols = lax.axis_size("col")
    me = my_row * cols + my_col

    def place(device):
        return (device // cols, lax.rem(device, cols))

    barrier = pltpu.get_barrier_semaphore()

    def greet(i, carry):
        pl.semaphore_signal(
            barrier, inc=1, device_id=place(lax.rem(me + i, DEVICES)), device_id_type=MESH
        )
        return carry

    def load(group, slot):
        return pltpu.make_async_copy(
            fringes.at[at(group * GROUP, GROUP), :], block.at[slot], load_sem.at[slot]
        )

    def send(source, target, device, index):
        @pl.when(device != me)
        def _():
            pltpu.make_async_remote_copy(
                src_ref=source, dst_ref=target, send_sem=send_sem.at[index],
                recv_sem=recv_sem.at[index], device_id=place(device), device_id_type=MESH,
            ).start()

        @pl.when(device == me)
        def _():
            pltpu.make_async_copy(source, target, own_sem.at[index]).start()


    def wait_recv(buffer, index):
        others = buffer.at[pl.ds(0, DEVICES - 1)]
        pltpu.make_async_copy(others, others, recv_sem.at[index]).wait()
        pltpu.make_async_copy(buffer.at[0], buffer.at[0], own_sem.at[index]).wait()

    def wait_send(buffer, index):
        others = buffer.at[pl.ds(0, DEVICES - 1)]
        pltpu.make_async_copy(others, others, send_sem.at[index]).wait()

    load(0, 0).start()
    lax.fori_loop(1, DEVICES, greet, 0)

    groups = HALF // GROUP
    for h in range(2):

        def group_step(g, carry, h=h):
            index = h * groups + g
            slot = lax.rem(index, 2)

            @pl.when(index < 2 * groups - 1)
            def _():
                load(index + 1, 1 - slot).start()

            load(index, slot).wait()

            def piece(i, inner):
                row_second(
                    mid.at[1 - slot], i // 2, lax.rem(i, 2), row_b, lobe, jnp.maximum(g - 1, 0)
                )
                for v in range(2):
                    for rows16 in range(2):
                        row_first(
                            block.at[slot], i * 2 + v, rows16, row_a, row_twist, mid.at[slot]
                        )
                return inner

            lax.fori_loop(0, 4, piece, 0)
            return carry

        lax.fori_loop(0, groups, group_step, 0)

        def last_piece(i, carry):
            row_second(mid.at[1], i // 2, lax.rem(i, 2), row_b, lobe, groups - 1)
            return carry

        lax.fori_loop(0, 4, last_piece, 0)

        if h == 0:
            pl.semaphore_wait(barrier, DEVICES - 1)

            def send_first(i, carry):
                k = lax.rem(me // 4 + i, 32)
                flipped = lobe[k].T
                for j in range(4):
                    send_a[k * 4 + j] = flipped[j * 64 : (j + 1) * 64]
                for j in range(4):
                    device = k * 4 + lax.rem(me + j, 4)
                    send(send_a.at[device], recv_a.at[me], device, 0)
                return carry

            lax.fori_loop(0, 32, send_first, 0)

            def send_zones(i, carry):
                device = lax.rem(me + i, DEVICES)
                send(zones.at[0], zones_out.at[me], device, 4)
                return carry

            lax.fori_loop(0, DEVICES, send_zones, 0)
        else:

            def send_second(i, carry):
                k = lax.rem(me // 4 + i, 32)
                flipped = lobe[k].T
                for j in range(4):
                    for chunk in range(2):
                        send_b[chunk, k * 4 + j] = flipped[
                            j * 64 + chunk * 32 : j * 64 + chunk * 32 + 32
                        ]
                for j in range(4):
                    device = k * 4 + lax.rem(me + j, 4)
                    send(send_b.at[0, device], recv_b.at[0, me], device, 1)
                return carry

            lax.fori_loop(0, 32, send_second, 0)

            def send_third(i, carry):
                device = lax.rem(me + i, DEVICES)
                send(send_b.at[1, device], recv_b.at[1, me], device, 2)
                return carry

            lax.fori_loop(0, DEVICES, send_third, 0)

    first_column = me // 4 + 32 * 32 * lax.rem(me, 4)
    wait_recv(recv_a, 0)
    for chunk in range(2):
        wait_recv(recv_b.at[chunk], 1 + chunk)

        def spread(i, carry, chunk=chunk):
            for u in range(8):
                a = i * 8 + u
                gather[0, at(a * 32, 32), :] = recv_a[a, chunk * 32 : chunk * 32 + 32, :].astype(f32)
                gather[1, at(a * 32, 32), :] = recv_b[chunk, a].astype(f32)
            return carry

        lax.fori_loop(0, DEVICES // 8, spread, 0)

        def pair_step(pair, carry, chunk=chunk):
            column_pair(
                pair, chunk, first_column, gather, (col_a, col_b, col_m, col_p),
                (col_twist, half_twist), edges, field,
            )
            return carry

        lax.fori_loop(0, 8, pair_step, 0)

        def send_field(i, carry, chunk=chunk):
            device = lax.rem(me + i, DEVICES)
            for part in range(2):
                send_c[chunk, device, part * 16 : part * 16 + 16, :] = field[
                    pl.ds(part * 128 + device, 16, stride=256), :
                ].astype(bf16)
            send(send_c.at[chunk, device], out.at[chunk, me], device, 5 + chunk)
            return carry

        lax.fori_loop(0, DEVICES, send_field, 0)

    wait_send(send_a, 0)
    wait_send(send_b.at[0], 1)
    wait_send(send_b.at[1], 2)
    wait_send(send_c.at[0], 5)
    wait_send(send_c.at[1], 6)
    wait_recv(out.at[0], 5)
    wait_recv(out.at[1], 6)
    wait_send(zones_out, 4)
    wait_recv(zones_out, 4)


def exchange(fringes, edges, zones, tables):
    names = ("row_a", "row_twist", "row_b", "col_a", "col_b", "col_m", "col_p", "col_twist", "half_twist")
    return pl.pallas_call(
        spectrum_kernel,
        out_shape=(
            jax.ShapeDtypeStruct((2, DEVICES, 32, KEPT), bf16),
            jax.ShapeDtypeStruct((DEVICES, 1, 128), f32),
        ),
        in_specs=[pl.BlockSpec(memory_space=pl.ANY)]
        + [pl.BlockSpec(memory_space=pltpu.VMEM)] * (2 + len(names)),
        out_specs=(pl.BlockSpec(memory_space=pl.ANY),) * 2,
        scratch_shapes=[
            pltpu.VMEM((2, GROUP, W), bf16),
            pltpu.VMEM((2, 2, 16 * GROUP, 2048), bf16),
            pltpu.VMEM((32, HALF, 256), bf16),
            pltpu.VMEM((DEVICES, 64, HALF), bf16),
            pltpu.VMEM((2, DEVICES, 32, HALF), bf16),
            pltpu.VMEM((DEVICES, 64, HALF), bf16),
            pltpu.VMEM((2, DEVICES, 32, HALF), bf16),
            pltpu.VMEM((2, DEVICES * 32, 128), f32),
            pltpu.VMEM((16 * 256, 128), f32),
            pltpu.VMEM((2, DEVICES, 32, KEPT), bf16),
            pltpu.SemaphoreType.DMA((2,)),
            pltpu.SemaphoreType.DMA((7,)),
            pltpu.SemaphoreType.DMA((7,)),
            pltpu.SemaphoreType.DMA((7,)),
        ],
        compiler_params=pltpu.CompilerParams(
            collective_id=0, has_side_effects=True, vmem_limit_bytes=60 << 20
        ),
        name="spectrum",
    )(fringes, edges, zones, *[tables[name] for name in names])


def height_kernel(zone_index, zone_table, received, pix_j, pix_twist, pix_k, out, rows, terms):
    group = pl.program_id(0)

    @pl.when(group == 0)
    def _():
        def flip(k, carry):
            stacked = jnp.concatenate(
                [received[chunk, k * 4 + j] for j in range(4) for chunk in range(2)], axis=0
            )
            rows[k] = stacked.T
            return carry

        lax.fori_loop(0, 32, flip, 0)

    left = rows[:, at(group * 16, 16), :].reshape(512, 256)

    def quarter(q, carry):
        for u in range(2):
            tile = q * 2 + u
            lanes = at(tile * 128, 128)
            mixed = dot(left, pix_j[:, at(tile * 256, 256)])
            for k0 in range(8):
                real = []
                imag = []
                for k1 in range(4):
                    k = k1 * 8 + k0
                    re = mixed[k * 16 : (k + 1) * 16, :128]
                    im = mixed[k * 16 : (k + 1) * 16, 128:]
                    if k:
                        cosine = pix_twist[k, 0, :, lanes]
                        sine = pix_twist[k, 1, :, lanes]
                        cosine = jnp.concatenate([cosine, cosine], axis=0)
                        sine = jnp.concatenate([sine, sine], axis=0)
                        re, im = re * cosine - im * sine, im * cosine + re * sine
                    real.append(re)
                    imag.append(im)
                even_re, even_im = real[0] + real[2], imag[0] + imag[2]
                odd_re, odd_im = real[1] + real[3], imag[1] + imag[3]
                gap_re, gap_im = real[0] - real[2], imag[0] - imag[2]
                side_re, side_im = real[1] - real[3], imag[1] - imag[3]
                results = (
                    (even_re + odd_re, even_im + odd_im),
                    (gap_re - side_im, gap_im + side_re),
                    (even_re - odd_re, even_im - odd_im),
                    (gap_re + side_im, gap_im - side_re),
                )
                for p0 in range(4):
                    for part in range(2):
                        terms[p0, pl.ds(k0 * 32 + part * 16, 16), u * 128 : u * 128 + 128] = results[
                            p0
                        ][part].astype(bf16)
        for p0 in range(4):
            mixed = dot(pix_k[p0], terms[p0])
            for p1 in range(8):
                p = p0 + 4 * p1
                real = mixed[p1 * 32 : p1 * 32 + 16]
                imag = mixed[p1 * 32 + 16 : p1 * 32 + 32]
                sine = imag * jnp.minimum(
                    lax.rsqrt(real * real + imag * imag), 1.0 / damping_floor
                )
                zone = zone_index[group, 2 * p + q // 2]
                source = zone // 32
                place = lax.rem(zone, 32)
                e0, e1, e2, e3 = (zone_table[source, place + 32 * r] for r in range(4))
                heights = e0 + sine * (e1 + sine * (e2 + sine * e3))
                out[:, at(1024 * p + q * 256, 256)] = heights.astype(bf16)
        return carry

    lax.fori_loop(0, 4, quarter, 0)


def height_map(zone_index, zone_table, received, tables):
    return pl.pallas_call(
        height_kernel,
        grid=(KEPT // ZB_R,),
        out_shape=jax.ShapeDtypeStruct((KEPT, W), bf16),
        in_specs=[pl.BlockSpec(memory_space=pltpu.SMEM)] * 2
        + [pl.BlockSpec(memory_space=pltpu.VMEM)] * 4,
        out_specs=pl.BlockSpec((ZB_R, W), lambda g: (g, 0)),
        scratch_shapes=[pltpu.VMEM((32, KEPT, 256), bf16), pltpu.VMEM((4, 256, 256), bf16)],
        compiler_params=pltpu.CompilerParams(vmem_limit_bytes=48 << 20),
        name="heights",
    )(zone_index, zone_table, received, tables["pix_j"], tables["pix_twist"], tables["pix_k"])


def body(tables, fringes, lobe_bounds, zone_index, zone_table):
    edges = jnp.repeat(lobe_bounds.T, 4, axis=1)
    zones = zone_table.reshape(1, 1, 128)
    received, zones = exchange(fringes, edges, zones, tables)
    return height_map(zone_index, zones.reshape(DEVICES, 128), received, tables)


def solution(mesh):
    placed = (P(("row", "col"), None), P(), P(("row", "col"), None), P(None, ("row", "col")))
    return jax.shard_map(
        functools.partial(body, make_tables()),
        mesh=mesh,
        in_specs=placed,
        out_specs=P(("row", "col"), None),
        check_vma=False,
    )
```

time: 764 us -> 150 us (0.20)
  the two profiles are of different devices: /device:TPU:16 before, /device:TPU:10 now
where the time goes in v1:
time: 150 us
  Pallas kernels  145 us (97%)
  local copies, waits for them, and re-layouts  5.22 us (3%)
    pallas_call x1, Pallas kernels, exchange(): pl.pallas_call(spectrum_kernel, out_shape=(jax.ShapeDtypeStruct((2, DEVIC...  109 us
    pallas_call x1, Pallas kernels, height_map(): pl.pallas_call(height_kernel, grid=(KEPT // ZB_R,), out_shape=jax.ShapeDt...  35.8 us

profile of v1, /device:TPU:10, one launch (start us, length us, event | category | flops | bytes accessed | tf_op | source)
XLA Modules:
  0.0 150.2 jit_solution(15349649060851121735)
XLA Ops:
  0.0 1.3 reshape.10.zones
  1.3 0.8 broadcast_in_dim.3
  2.1 0.7 reshape.9.edges
  2.8 0.0 copy-start
  2.8 0.0 copy-start.2
  2.8 0.0 copy-start.3
  2.8 0.0 copy-start.5
  2.8 109.1 %spectrum.1 = (bf16[2,128,32,128]{3,2,1,0:T(8,128)(2,1)}, f32[128,1,128]{2,1,0:T(1,128)}) custom-call(bf16[256,32768]{1,0:T(8,128)(2,1)} %fringes.1, s32[2,256]{1,0:T(2,128)} %reshape.9.edges, f32[1,1,128]{2,1,0:T(1,128)} %reshape.10.zones, bf16[256,256]{1,0:T(8,128)(2,1)} %constant.22.clone.row_a, f32[16,2,8,2048]{3,2,1,0:T(8,128)} %constant.23.clone.row_twist, ...), custom_call_target="tpu_custom_call" | custom-call | tf_op jit(solution)/shard_map/spectrum/pallas_call | solution.py:399
  111.9 0.0 copy-done
  111.9 0.0 copy-done.2
  112.0 0.0 copy-done.3
  112.0 0.0 copy-done.5
  112.0 0.0 copy-start.1
  112.0 1.6 %copy-done.1 = bf16[2,128,32,128]{3,2,1,0:T(8,128)(2,1)S(1)} copy-done((bf16[2,128,32,128]{3,2,1,0:T(8,128)(2,1)S(1)}, bf16[2,128,32,128]{3,2,1,0:T(8,128)(2,1)}, u32[]{:S(2)}) %copy-start.1) | copy-done | bytes 2097176
  113.6 0.0 copy-start.4
  113.6 0.8 copy-done.4
  114.4 35.8 %heights.1 = bf16[128,32768]{1,0:T(8,128)(2,1)} custom-call(s32[8,64]{1,0:T(8,128)S(1)} %copy-done.5, f32[128,128]{1,0:T(8,128)S(1)} %bitcast.2, bf16[2,128,32,128]{3,2,1,0:T(8,128)(2,1)S(1)} %copy-done.1, bf16[256,2048]{1,0:T(8,128)(2,1)S(1)} %copy-done.2, f32[32,2,8,1024]{3,2,1,0:T(8,128)S(1)} %copy-done, bf16[4,256,256]{2,1,0:T(8,128)(2,1)S(1)} %copy-done.3), custom_call_target="tpu_custom_call" | custom-call | tf_op jit(solution)/shard_map/heights/pallas_call | solution.py:503
Async XLA Ops:
  2.8 109.2 %copy-start = (f32[32,2,8,1024]{3,2,1,0:T(8,128)S(1)}, f32[32,2,8,1024]{3,2,1,0:T(8,128)}, u32[]{:S(2)}) copy-start(f32[32,2,8,1024]{3,2,1,0:T(8,128)} %constant.31.clone.pix_twist) | copy-start | bytes 6291460
  2.8 109.2 %copy-start.2 = (bf16[256,2048]{1,0:T(8,128)(2,1)S(1)}, bf16[256,2048]{1,0:T(8,128)(2,1)}, u32[]{:S(2)}) copy-start(bf16[256,2048]{1,0:T(8,128)(2,1)} %constant.30.clone.pix_j) | copy-start | bytes 3145732
  2.8 109.2 %copy-start.3 = (bf16[4,256,256]{2,1,0:T(8,128)(2,1)S(1)}, bf16[4,256,256]{2,1,0:T(8,128)(2,1)}, u32[]{:S(2)}) copy-start(bf16[4,256,256]{2,1,0:T(8,128)(2,1)} %constant.32.clone.pix_k) | copy-start | bytes 1572868
  2.8 109.2 %copy-start.5 = (s32[8,64]{1,0:T(8,128)S(1)}, s32[8,64]{1,0:T(8,128)}, u32[]{:S(2)}) copy-start(s32[8,64]{1,0:T(8,128)} %zone_index.1) | copy-start | bytes 6148
  112.0 1.6 %copy-start.1 = (bf16[2,128,32,128]{3,2,1,0:T(8,128)(2,1)S(1)}, bf16[2,128,32,128]{3,2,1,0:T(8,128)(2,1)}, u32[]{:S(2)}) copy-start(bf16[2,128,32,128]{3,2,1,0:T(8,128)(2,1)} %get-tuple-element.8.received) | copy-start | bytes 6291460
  113.6 0.8 copy-start.4

commit v2 on v1

v2 whole, which is shorter than its diff:
```python
import functools
import math

import jax
import jax.numpy as jnp
import ml_dtypes
import numpy as np
from jax import lax
from jax.experimental import pallas as pl
from jax.experimental.pallas import tpu as pltpu
from jax.sharding import PartitionSpec as P

W = 32768
H = 32768
LOBE = 4096
LOBE_START = 4096
DEVICES = 128
ROWS = H // DEVICES
HALF = ROWS // 2
KEPT = H // (2 * DEVICES)
GROUP = 32
ZB_R = 16

damping_floor = 0.5
bf16 = jnp.bfloat16
f32 = jnp.float32
MESH = pl.DeviceIdType.MESH


def turns(first, second, period):
    angles = (np.outer(first, second) % period).astype(np.float64) * (2.0 * math.pi / period)
    return np.cos(angles), np.sin(angles)


def lane_tiles(matrix):
    shape = matrix.shape
    return np.moveaxis(matrix.reshape(*shape[:-1], shape[-1] // 128, 128), -2, -3)


def by_tile(rows):
    first, two, length = rows.shape
    return np.broadcast_to(
        rows.reshape(first, two, length // 128, 1, 128), (first, two, length // 128, 8, 128)
    )


def make_tables():
    n4, n8, n16, n32 = (np.arange(n) for n in (4, 8, 16, 32))
    n128, n256, n1024, n2048 = (np.arange(n) for n in (128, 256, 1024, 2048))
    half = {}
    full = {}
    cosine, sine = turns(n16, n16, 16)
    half["row_a"] = np.kron(np.concatenate([cosine[:9], -sine[1:8]], 0), np.eye(16))
    cosine, sine = turns(n16, n2048, W)
    full["row_twist"] = by_tile(np.stack([cosine, sine], 1))
    sides = []
    for odd in range(2):
        cosine, sine = turns(n1024, LOBE_START // 16 + 2 * n128 + odd, 2048)
        real = np.concatenate([cosine, sine], 0).reshape(2048, 4, 2, 16)
        imag = np.concatenate([-sine, cosine], 0).reshape(2048, 4, 2, 16)
        sides.append(np.stack([real, imag], 3).transpose(0, 2, 1, 3, 4).reshape(2048, 256))
    half["row_b"] = np.stack(sides)
    cosine, sine = turns(n128, n128, 128)
    half["col_a"] = np.block([[cosine, sine], [-sine, cosine]])
    half["col_m"] = np.block([[cosine, sine], [-sine, cosine]])
    half["col_p"] = np.block([[cosine, -sine], [sine, cosine]])
    cosine, sine = turns(n128, n256, H)
    full["col_twist"] = np.stack([cosine, sine])
    cosine, sine = turns(n256, n256, 256)
    half["col_b"] = np.block([[cosine, -sine], [sine, cosine]])
    cosine, sine = turns(n128, n128, H // 2)
    full["half_twist"] = np.stack([cosine, sine])
    cosine, sine = turns(n128, n1024, 1024)
    real = np.stack([cosine.reshape(128, 8, 128), sine.reshape(128, 8, 128)], 2).reshape(128, 2048)
    imag = np.stack([-sine.reshape(128, 8, 128), cosine.reshape(128, 8, 128)], 2).reshape(128, 2048)
    half["pix_j"] = np.stack([real.reshape(4, 2, 16, 2048), imag.reshape(4, 2, 16, 2048)], 2).reshape(
        256, 2048
    )
    cosine, sine = turns(n32, n1024, W)
    full["pix_twist"] = by_tile(np.stack([cosine, sine], 1))
    mats = []
    for p0 in range(4):
        cosine, sine = turns(p0 + 4 * n8, n8, 32)
        block = np.stack(
            [np.stack([cosine, -sine], -1), np.stack([sine, cosine], -1)], 1
        ).reshape(16, 16)
        mats.append(np.kron(block, np.eye(16)))
    half["pix_k"] = np.stack(mats)
    made = {name: lane_tiles(value).astype(ml_dtypes.bfloat16) for name, value in half.items()}
    made.update({name: np.ascontiguousarray(value, np.float32) for name, value in full.items()})
    return made


def dot(left, right):
    return jnp.dot(left, right, preferred_element_type=f32)


def joined(tiles):
    return jnp.concatenate([tiles[i] for i in range(tiles.shape[0])], axis=1)


def at(start, size):
    return pl.ds(pl.multiple_of(start, size), size)


def row_first(block, pair, rows16, mat, twist, mid):
    sides = [
        [
            block[pl.ds(rows16 * 16, 16), at(2048 * a + 1024 * upper + pair * 256, 256)]
            for a in range(16)
        ]
        for upper in range(2)
    ]
    left = joined(mat)
    rows = [pl.ds(k * GROUP + rows16 * 16, 16) for k in range(16)]
    for v in range(2):
        tile = pair * 2 + v
        right = jnp.concatenate(
            [
                jnp.concatenate([piece[:, v * 128 : v * 128 + 128] for piece in side], axis=0)
                for side in sides
            ],
            axis=1,
        )
        mixed = dot(left, right)

        def part(index, upper):
            return mixed[index * 16 : (index + 1) * 16, upper * 128 : (upper + 1) * 128]

        def factor(k, index, upper):
            value = twist[k, index, upper * 8 + tile]
            return jnp.concatenate([value, value], axis=0)

        for k in range(16):
            twisted = []
            for upper in range(2):
                source = k if k <= 8 else 16 - k
                real = part(source, upper)
                if k == 0:
                    twisted.append((real, None))
                    continue
                cosine = factor(k, 0, upper)
                sine = factor(k, 1, upper)
                if k == 8:
                    twisted.append((real * cosine, -(real * sine)))
                    continue
                imag = part(source + 8, upper)
                if k < 8:
                    twisted.append((real * cosine + imag * sine, imag * cosine - real * sine))
                else:
                    twisted.append((real * cosine - imag * sine, -(imag * cosine + real * sine)))
            (real0, imag0), (real1, imag1) = twisted
            mid[0, tile, rows[k], :] = (real0 + real1).astype(bf16)
            mid[1, tile, rows[k], :] = (real0 - real1).astype(bf16)
            if imag0 is None:
                mid[0, 8 + tile, rows[k], :] = jnp.zeros((16, 128), bf16)
                mid[1, 8 + tile, rows[k], :] = jnp.zeros((16, 128), bf16)
            else:
                mid[0, 8 + tile, rows[k], :] = (imag0 + imag1).astype(bf16)
                mid[1, 8 + tile, rows[k], :] = (imag0 - imag1).astype(bf16)


def row_second(mid, odd, block, mat, lobe, group):
    rows = 8 * GROUP
    left = jnp.concatenate([mid[odd, t, at(block * rows, rows), :] for t in range(16)], axis=1)
    mixed = dot(left, joined(mat.at[odd])).astype(bf16)
    for k in range(8):
        for chunk in range(2):
            lobe[odd * 16 + block * 8 + k, chunk, at(group * GROUP, GROUP), :] = mixed[
                k * GROUP : (k + 1) * GROUP, chunk * 128 : chunk * 128 + 128
            ]


def column_pair(pair, chunk, first_column, gather, mats, twists, edges, field):
    col_a, col_b, col_m, col_p = mats
    col_twist, half_twist = twists
    middles = []
    for u in range(2):
        j = pair * 2 + u
        parts = []
        for part in range(2):
            parts.append(
                jnp.concatenate(
                    [gather[h, pl.ds(part * 16 + j, DEVICES, stride=32), :] for h in range(2)],
                    axis=1,
                )
            )
        mixed = dot(joined(col_a), jnp.concatenate(parts, axis=0).astype(bf16))
        real, imag = mixed[:128], mixed[128:]
        cosine, sine = col_twist[0], col_twist[1]
        middles.append(
            jnp.concatenate(
                [
                    (real * cosine + imag * sine).astype(bf16),
                    (imag * cosine - real * sine).astype(bf16),
                ],
                axis=1,
            )
        )
    spectrum = dot(jnp.concatenate(middles, axis=0), joined(col_b))
    folded = []
    for u in range(2):
        column = first_column + 32 * (chunk * 16 + pair * 2 + u)
        keep = jnp.where((column >= edges[0]) & (column < edges[1]), 1.0 / (H * W), 0.0)
        rows = spectrum[u * 128 : (u + 1) * 128]
        folded.append(
            jnp.concatenate(
                [
                    (
                        rows[:, part * 256 : part * 256 + 128] * keep[:, :128]
                        + rows[:, part * 256 + 128 : part * 256 + 256] * keep[:, 128:]
                    ).astype(bf16)
                    for part in range(2)
                ],
                axis=1,
            )
        )
    halves = dot(jnp.concatenate(folded, axis=0), joined(col_m))
    cosine, sine = half_twist[0], half_twist[1]
    terms = []
    for u in range(2):
        rows = halves[u * 128 : (u + 1) * 128]
        real, imag = rows[:, :128], rows[:, 128:]
        terms.append(
            jnp.concatenate(
                [
                    (real * cosine - imag * sine).astype(bf16),
                    (imag * cosine + real * sine).astype(bf16),
                ],
                axis=0,
            )
        )
    out = dot(joined(col_p), jnp.concatenate(terms, axis=1))
    for u in range(2):
        field[at((pair * 2 + u) * 256, 256), :] = out[:, u * 128 : (u + 1) * 128]


def spectrum_kernel(
    bounds, fringes, zones, *refs,
):
    given, refs = refs[:9], refs[9:]
    out, zones_out, *refs = refs
    tables, refs = refs[:9], refs[9:]
    row_a, row_twist, row_b, col_a, col_b, col_m, col_p, col_twist, half_twist = tables
    block, mid, lobe, send_a, recv_a, gather, field, send_c, edges, zone_rows, zone_row = refs[:11]
    load_sem, send_sem, recv_sem, own_sem, table_sem = refs[11:]
    table_copies = [
        pltpu.make_async_copy(given[i], tables[i], table_sem.at[i]) for i in range(9)
    ]
    my_row = lax.axis_index("row")
    my_col = lax.axis_index("col")
    cols = lax.axis_size("col")
    me = my_row * cols + my_col

    def place(device):
        return (lax.div(device, cols), lax.rem(device, cols))

    def other(i):
        return lax.rem(me + i, DEVICES)

    barrier = pltpu.get_barrier_semaphore()

    def greet(i, carry):
        pl.semaphore_signal(barrier, inc=1, device_id=place(other(i)), device_id_type=MESH)
        return carry

    def load(group, slot):
        return pltpu.make_async_copy(
            fringes.at[at(group * GROUP, GROUP), :], block.at[slot], load_sem.at[slot]
        )

    def send(source, target, device, index):
        pltpu.make_async_remote_copy(
            src_ref=source, dst_ref=target, send_sem=send_sem.at[index],
            recv_sem=recv_sem.at[index], device_id=place(device), device_id_type=MESH,
        ).start()

    def keep(source, target, index):
        pltpu.make_async_copy(source, target, own_sem.at[index]).start()

    def wait_recv(buffer, index):
        others = buffer.at[pl.ds(0, DEVICES - 1)]
        pltpu.make_async_copy(others, others, recv_sem.at[index]).wait()
        pltpu.make_async_copy(buffer.at[0], buffer.at[0], own_sem.at[index]).wait()

    def wait_send(buffer, index):
        others = buffer.at[pl.ds(0, DEVICES - 1)]
        pltpu.make_async_copy(others, others, send_sem.at[index]).wait()

    load(0, 0).start()
    for copy in table_copies:
        copy.start()
    lax.fori_loop(1, DEVICES, greet, 0)

    lanes = lax.broadcasted_iota(jnp.int32, (1, 256), 1)

    def edge_step(t, carry):
        mine = (lanes >= 4 * t) & (lanes < 4 * t + 4)
        return tuple(jnp.where(mine, bounds[side, t], carry[side]) for side in range(2))

    both = lax.fori_loop(0, 64, edge_step, (jnp.zeros((1, 256), jnp.int32),) * 2)
    edges[0] = both[0]
    edges[1] = both[1]
    zone_rows[...] = jnp.zeros((8, 128), f32)
    zone_rows[0:4, 0:32] = zones[...]
    spread_rows = zone_rows[...]
    zone_row[...] = spread_rows[0:1] + sum(
        pltpu.roll(spread_rows, 32 * r, 1)[r : r + 1] for r in range(1, 4)
    )

    table_copies[0].wait()
    table_copies[1].wait()

    def first_only(group):
        slot = lax.rem(group, 2)
        load(group + 1, 1 - slot).start()
        load(group, slot).wait()

        def piece(pair, carry):
            for rows16 in range(2):
                row_first(block.at[slot], pair, rows16, row_a, row_twist, mid.at[slot])
            return carry

        lax.fori_loop(0, 4, piece, 0)

    def both_steps(group, last):
        slot = lax.rem(group, 2)
        if not last:
            load(group + 1, 1 - slot).start()
        load(group, slot).wait()

        def piece(i, carry):
            row_second(
                mid.at[1 - slot], lax.div(i, 2), lax.rem(i, 2), row_b, lobe, lax.rem(group - 1, 4)
            )
            for rows16 in range(2):
                row_first(block.at[slot], i, rows16, row_a, row_twist, mid.at[slot])
            return carry

        lax.fori_loop(0, 4, piece, 0)

    def second_only(group):
        slot = lax.rem(group, 2)

        def piece(i, carry):
            row_second(mid.at[slot], lax.div(i, 2), lax.rem(i, 2), row_b, lobe, lax.rem(group, 4))
            return carry

        lax.fori_loop(0, 4, piece, 0)

    def send_block(buffer, target, k, low, index):
        for j in range(low, 4):
            device = k * 4 + lax.rem(me + j, 4)
            send(buffer.at[device], target.at[me], device, index)

    def quarter_step(c, carry):
        first_only(2 * c)

        @pl.when(c == 0)
        def _():
            table_copies[2].wait()

        both_steps(2 * c + 1, False)
        second_only(2 * c + 1)

        @pl.when(c == 0)
        def _():
            pl.semaphore_wait(barrier, DEVICES - 1)

        def pack(i):
            k = lax.rem(lax.div(me, 4) + i, 32)
            rows = at(c * 64, 64)
            upper = lobe[k, c, rows, :]
            lower = lobe[k, 1 - c, rows, :]
            flipped = jnp.concatenate([upper, lower], axis=0).T
            for j in range(4):
                send_a[c, k * 4 + j] = flipped[j * 32 : (j + 1) * 32]
            return k

        k = pack(0)
        keep(send_a.at[c, me], recv_a.at[c, me], c)
        send_block(send_a.at[c], recv_a.at[c], k, 1, c)

        def pack_step(i, inner):
            send_block(send_a.at[c], recv_a.at[c], pack(i), 0, c)
            return inner

        lax.fori_loop(1, 32, pack_step, 0)
        return carry

    lax.fori_loop(0, 2, quarter_step, 0)

    keep(zone_row, zones_out.at[me], 4)

    def send_zones(i, carry):
        send(zone_row, zones_out.at[me], other(i), 4)
        return carry

    first_only(4)

    def half_step(g, carry):
        both_steps(g, False)
        return carry

    lax.fori_loop(5, 7, half_step, 0)
    both_steps(7, True)
    second_only(7)

    def pack_half(i):
        k = lax.rem(lax.div(me, 4) + i, 32)
        for chunk in range(2):
            flipped = lobe[k, chunk].T
            for j in range(4):
                send_a[2 + chunk, k * 4 + j] = flipped[j * 32 : (j + 1) * 32]
        return k

    k = pack_half(0)
    keep(send_a.at[2, me], recv_a.at[2, me], 2)
    send_block(send_a.at[2], recv_a.at[2], k, 1, 2)

    def pack_half_step(i, carry):
        send_block(send_a.at[2], recv_a.at[2], pack_half(i), 0, 2)
        return carry

    lax.fori_loop(1, 32, pack_half_step, 0)
    keep(send_a.at[3, me], recv_a.at[3, me], 3)

    def send_last(i, carry):
        send(send_a.at[3, other(i)], recv_a.at[3, me], other(i), 3)
        return carry

    lax.fori_loop(1, DEVICES, send_last, 0)
    lax.fori_loop(1, DEVICES, send_zones, 0)

    first_column = lax.div(me, 4) + 32 * 32 * lax.rem(me, 4)
    low_lanes = lax.broadcasted_iota(jnp.int32, (32, 128), 1) < 64
    for copy in table_copies[3:]:
        copy.wait()
    wait_recv(recv_a.at[0], 0)
    wait_recv(recv_a.at[1], 1)
    for chunk in range(2):
        wait_recv(recv_a.at[2 + chunk], 2 + chunk)

        def spread(i, carry, chunk=chunk):
            for u in range(8):
                a = i * 8 + u
                early = recv_a[0, a].astype(f32)
                late = recv_a[1, a].astype(f32)
                if chunk == 0:
                    mine = jnp.where(low_lanes, early, late)
                else:
                    mine = pltpu.roll(jnp.where(low_lanes, late, early), 64, 1)
                gather[0, at(a * 32, 32), :] = mine
                gather[1, at(a * 32, 32), :] = recv_a[2 + chunk, a].astype(f32)
            return carry

        lax.fori_loop(0, DEVICES // 8, spread, 0)

        def pair_step(pair, carry, chunk=chunk):
            column_pair(
                pair, chunk, first_column, gather, (col_a, col_b, col_m, col_p),
                (col_twist, half_twist), edges, field,
            )
            return carry

        lax.fori_loop(0, 8, pair_step, 0)

        def pack_field(i, chunk=chunk):
            device = other(i)
            for part in range(2):
                send_c[chunk, device, part * 16 : part * 16 + 16, :] = field[
                    pl.ds(part * 128 + device, 16, stride=256), :
                ].astype(bf16)
            return device

        def send_field(i, chunk=chunk):
            device = pack_field(i)
            send(send_c.at[chunk, device], out.at[chunk, me], device, 5 + chunk)

        pack_field(0)
        keep(send_c.at[chunk, me], out.at[chunk, me], 5 + chunk)
        for i in range(1, 4):
            send_field(i)

        def field_step(i, carry, chunk=chunk):
            for u in range(4):
                send_field(i * 4 + u)
            return carry

        lax.fori_loop(1, DEVICES // 4, field_step, 0)

    for index in range(4):
        wait_send(send_a.at[index], index)
    wait_send(zones_out, 4)
    wait_recv(zones_out, 4)
    for chunk in range(2):
        wait_send(send_c.at[chunk], 5 + chunk)
        wait_recv(out.at[chunk], 5 + chunk)


def exchange(lobe_bounds, fringes, zones, tables):
    names = ("row_a", "row_twist", "row_b", "col_a", "col_b", "col_m", "col_p", "col_twist", "half_twist")
    constants = [tables[name] for name in names]
    return pl.pallas_call(
        spectrum_kernel,
        out_shape=(
            jax.ShapeDtypeStruct((2, DEVICES, 32, KEPT), bf16),
            jax.ShapeDtypeStruct((DEVICES, 1, 128), f32),
        ),
        in_specs=[
            pl.BlockSpec(memory_space=pltpu.SMEM),
            pl.BlockSpec(memory_space=pltpu.HBM),
            pl.BlockSpec(memory_space=pltpu.VMEM),
        ]
        + [pl.BlockSpec(memory_space=pltpu.HBM)] * len(names),
        out_specs=(pl.BlockSpec(memory_space=pltpu.HBM),) * 2,
        scratch_shapes=[pltpu.VMEM(value.shape, value.dtype) for value in constants]
        + [
            pltpu.VMEM((2, GROUP, W), bf16),
            pltpu.VMEM((2, 2, 16, 16 * GROUP, 128), bf16),
            pltpu.VMEM((32, 2, HALF, 128), bf16),
            pltpu.VMEM((4, DEVICES, 32, 128), bf16),
            pltpu.VMEM((4, DEVICES, 32, 128), bf16),
            pltpu.VMEM((2, DEVICES * 32, 128), f32),
            pltpu.VMEM((16 * 256, 128), f32),
            pltpu.VMEM((2, DEVICES, 32, KEPT), bf16),
            pltpu.VMEM((2, 1, 256), jnp.int32),
            pltpu.VMEM((8, 128), f32),
            pltpu.VMEM((1, 128), f32),
            pltpu.SemaphoreType.DMA((2,)),
            pltpu.SemaphoreType.DMA((7,)),
            pltpu.SemaphoreType.DMA((7,)),
            pltpu.SemaphoreType.DMA((7,)),
            pltpu.SemaphoreType.DMA((9,)),
        ],
        compiler_params=pltpu.CompilerParams(
            collective_id=0, has_side_effects=True, vmem_limit_bytes=60 << 20
        ),
        name="spectrum",
    )(lobe_bounds, fringes, zones, *constants)


def pixel_first(left, tile, half, pix_j, pix_twist, terms):
    mixed = dot(left, jnp.concatenate([pix_j[tile * 2], pix_j[tile * 2 + 1]], axis=1))
    for k0 in range(8):
        real = []
        imag = []
        for k1 in range(4):
            k = k1 * 8 + k0
            re = mixed[k * 16 : (k + 1) * 16, :128]
            im = mixed[k * 16 : (k + 1) * 16, 128:]
            if k:
                cosine = pix_twist[k, 0, tile]
                sine = pix_twist[k, 1, tile]
                cosine = jnp.concatenate([cosine, cosine], axis=0)
                sine = jnp.concatenate([sine, sine], axis=0)
                re, im = re * cosine - im * sine, im * cosine + re * sine
            real.append(re)
            imag.append(im)
        even_re, even_im = real[0] + real[2], imag[0] + imag[2]
        odd_re, odd_im = real[1] + real[3], imag[1] + imag[3]
        gap_re, gap_im = real[0] - real[2], imag[0] - imag[2]
        side_re, side_im = real[1] - real[3], imag[1] - imag[3]
        results = (
            (even_re + odd_re, even_im + odd_im),
            (gap_re - side_im, gap_im + side_re),
            (even_re - odd_re, even_im - odd_im),
            (gap_re + side_im, gap_im - side_re),
        )
        for p0 in range(4):
            for part in range(2):
                terms[p0, half, pl.ds(k0 * 32 + part * 16, 16), :] = results[p0][part].astype(bf16)


def pixel_second(group, q, pix_k, terms, zone_index, zone_table, pixels):
    for p0 in range(4):
        left = joined(pix_k.at[p0])
        mixed = [dot(left, joined(terms.at[u, p0])) for u in range(2)]
        for p1 in range(8):
            p = p0 + 4 * p1
            zone = zone_index[group, 2 * p + q // 2]
            source = lax.shift_right_logical(zone, 5)
            place = lax.bitwise_and(zone, 31)
            e0, e1, e2, e3 = (zone_table[source, place + 32 * r] for r in range(4))
            for u in range(2):
                real = mixed[u][p1 * 32 : p1 * 32 + 16]
                imag = mixed[u][p1 * 32 + 16 : p1 * 32 + 32]
                sine = imag * jnp.minimum(lax.rsqrt(real * real + imag * imag), 1.0 / damping_floor)
                heights = e0 + sine * (e1 + sine * (e2 + sine * e3))
                for h in range(2):
                    pixels[h * 8 : h * 8 + 8, pl.ds(1024 * p + (q + u) * 256, 256)] = heights[
                        h * 8 : h * 8 + 8
                    ].astype(bf16)


def height_kernel(
    zone_index, zone_table, received_in, pix_j_in, pix_twist_in, pix_k_in, out,
    received, pix_j, pix_twist, pix_k, rows, terms, pixels, store_sem, load_sem,
):
    loads = [
        pltpu.make_async_copy(source, target, load_sem.at[i])
        for i, (source, target) in enumerate(
            ((received_in, received), (pix_j_in, pix_j), (pix_twist_in, pix_twist), (pix_k_in, pix_k))
        )
    ]
    for copy in loads:
        copy.start()
    loads[0].wait()

    def flip(i, carry):
        for u in range(2):
            k = i * 2 + u
            for half in range(2):
                stacked = jnp.concatenate(
                    [
                        received[chunk, k * 4 + half * 2 + j]
                        for j in range(2)
                        for chunk in range(2)
                    ],
                    axis=0,
                )
                rows[k, half] = stacked.T
        return carry

    lax.fori_loop(0, 16, flip, 0)
    for copy in loads[1:]:
        copy.wait()
    groups = KEPT // ZB_R

    def store(group):
        slot = lax.rem(group, 2)
        return pltpu.make_async_copy(
            pixels.at[slot], out.at[at(group * ZB_R, ZB_R), :], store_sem.at[slot]
        )

    def front(group):
        left = jnp.concatenate(
            [rows[:, half, at(group * 16, 16), :].reshape(512, 128) for half in range(2)], axis=1
        )
        for q in range(4):
            for half in range(2):
                pixel_first(
                    left, q * 2 + half, half, pix_j, pix_twist, terms.at[lax.rem(group, 2), q]
                )

    def back(group):
        slot = lax.rem(group, 2)

        @pl.when(group >= 2)
        def _():
            store(group - 2).wait()

        for q in range(0, 4, 2):
            pixel_second(
                group, q, pix_k, terms.at[slot, pl.ds(q, 2)], zone_index, zone_table, pixels.at[slot]
            )

    front(0)

    def step(group, carry):
        back(group - 1)
        front(group)
        store(group - 1).start()
        return carry

    lax.fori_loop(1, groups, step, 0)
    back(groups - 1)
    store(groups - 1).start()
    store(groups - 2).wait()
    store(groups - 1).wait()


def height_map(zone_index, zone_table, received, tables):
    constants = [tables[name] for name in ("pix_j", "pix_twist", "pix_k")]
    return pl.pallas_call(
        height_kernel,
        out_shape=jax.ShapeDtypeStruct((KEPT, W), bf16),
        in_specs=[pl.BlockSpec(memory_space=pltpu.SMEM)] * 2
        + [pl.BlockSpec(memory_space=pltpu.HBM)] * 4,
        out_specs=pl.BlockSpec(memory_space=pltpu.HBM),
        scratch_shapes=[pltpu.VMEM(received.shape, received.dtype)]
        + [pltpu.VMEM(value.shape, value.dtype) for value in constants]
        + [
            pltpu.VMEM((32, 2, KEPT, 128), bf16),
            pltpu.VMEM((2, 4, 4, 2, 256, 128), bf16),
            pltpu.VMEM((2, ZB_R, W), bf16),
            pltpu.SemaphoreType.DMA((2,)),
            pltpu.SemaphoreType.DMA((4,)),
        ],
        compiler_params=pltpu.CompilerParams(vmem_limit_bytes=60 << 20),
        name="heights",
    )(zone_index, zone_table, received, *constants)


def body(tables, fringes, lobe_bounds, zone_index, zone_table):
    received, zones = exchange(lobe_bounds.T, fringes, zone_table, tables)
    return height_map(zone_index, zones.reshape(DEVICES, 128), received, tables)


def solution(mesh):
    placed = (P(("row", "col"), None), P(), P(("row", "col"), None), P(None, ("row", "col")))
    return jax.shard_map(
        functools.partial(body, make_tables()),
        mesh=mesh,
        in_specs=placed,
        out_specs=P(("row", "col"), None),
        check_vma=False,
    )
```

time: 150 us -> 124 us (0.83)
  the two profiles are of different devices: /device:TPU:10 before, /device:TPU:2 now
where the time goes in v2:
time: 124 us
  Pallas kernels  124 us (100%)
    pallas_call x1, Pallas kernels, exchange(): pl.pallas_call(spectrum_kernel, out_shape=(jax.ShapeDtypeStruct((2, DEVIC...  102 us
    pallas_call x1, Pallas kernels, height_map(): pl.pallas_call(height_kernel, out_shape=jax.ShapeDtypeStruct((KEPT, W), b...  22.4 us

profile of v2, /device:TPU:2, one launch (start us, length us, event | category | flops | bytes accessed | tf_op | source)
XLA Modules:
  0.0 124.2 jit_solution(13551935829473049888)
XLA Ops:
  0.0 101.8 %spectrum.1 = (bf16[2,128,32,128]{3,2,1,0:T(8,128)(2,1)}, f32[128,1,128]{2,1,0:T(1,128)}) custom-call(s32[2,64]{1,0:T(2,128)} %bitcast.3, bf16[256,32768]{1,0:T(8,128)(2,1)} %fringes.1, f32[4,32]{1,0:T(4,128)} %zones.1, bf16[2,256,128]{2,1,0:T(8,128)(2,1)} %constant.22.clone.refs_0_, f32[16,2,16,8,128]{4,3,2,1,0:T(8,128)} %constant.23.clone.refs_1_, ...), custom_call_target="tpu_custom_call" | custom-call | tf_op jit(solution)/shard_map/spectrum/pallas_call | solution.py:504
  101.8 22.4 %heights.1 = bf16[128,32768]{1,0:T(8,128)(2,1)} custom-call(s32[8,64]{1,0:T(8,128)} %zone_index.1, f32[128,128]{1,0:T(8,128)} %bitcast.2, bf16[2,128,32,128]{3,2,1,0:T(8,128)(2,1)} %get-tuple-element.8.received_in, bf16[16,256,128]{2,1,0:T(8,128)(2,1)} %constant.30.clone.pix_j_in, f32[32,2,8,8,128]{4,3,2,1,0:T(8,128)} %constant.31.clone.pix_twist_in, ...), custom_call_target="tpu_custom_call" | custom-call | tf_op jit(solution)/shard_map/heights/pallas_call | solution.py:675

commit v3 on v2

--- a/solution.py
+++ b/solution.py
@@ -19,6 +19,7 @@
 HALF = ROWS // 2
 KEPT = H // (2 * DEVICES)
 GROUP = 32
+COLUMNS = 4
 ZB_R = 16
 
 damping_floor = 0.5
@@ -171,12 +172,12 @@
             ]
 
 
-def column_pair(pair, chunk, first_column, gather, mats, twists, edges, field):
+def column_set(index, chunk, first_column, gather, mats, twists, edges, field):
     col_a, col_b, col_m, col_p = mats
     col_twist, half_twist = twists
-    middles = []
-    for u in range(2):
-        j = pair * 2 + u
+    inputs = []
+    for u in range(COLUMNS):
+        j = index * COLUMNS + u
         parts = []
         for part in range(2):
             parts.append(
@@ -185,8 +186,12 @@
                     axis=1,
                 )
             )
-        mixed = dot(joined(col_a), jnp.concatenate(parts, axis=0).astype(bf16))
-        real, imag = mixed[:128], mixed[128:]
+        inputs.append(jnp.concatenate(parts, axis=0).astype(bf16))
+    mixed = dot(joined(col_a), jnp.concatenate(inputs, axis=1))
+    middles = []
+    for u in range(COLUMNS):
+        lanes = slice(u * 256, (u + 1) * 256)
+        real, imag = mixed[:128, lanes], mixed[128:, lanes]
         cosine, sine = col_twist[0], col_twist[1]
         middles.append(
             jnp.concatenate(
@@ -199,8 +204,8 @@
         )
     spectrum = dot(jnp.concatenate(middles, axis=0), joined(col_b))
     folded = []
-    for u in range(2):
-        column = first_column + 32 * (chunk * 16 + pair * 2 + u)
+    for u in range(COLUMNS):
+        column = first_column + 32 * (chunk * 16 + index * COLUMNS + u)
         keep = jnp.where((column >= edges[0]) & (column < edges[1]), 1.0 / (H * W), 0.0)
         rows = spectrum[u * 128 : (u + 1) * 128]
         folded.append(
@@ -218,7 +223,7 @@
     halves = dot(jnp.concatenate(folded, axis=0), joined(col_m))
     cosine, sine = half_twist[0], half_twist[1]
     terms = []
-    for u in range(2):
+    for u in range(COLUMNS):
         rows = halves[u * 128 : (u + 1) * 128]
         real, imag = rows[:, :128], rows[:, 128:]
         terms.append(
@@ -231,8 +236,8 @@
             )
         )
     out = dot(joined(col_p), jnp.concatenate(terms, axis=1))
-    for u in range(2):
-        field[at((pair * 2 + u) * 256, 256), :] = out[:, u * 128 : (u + 1) * 128]
+    for u in range(COLUMNS):
+        field[at((index * COLUMNS + u) * 256, 256), :] = out[:, u * 128 : (u + 1) * 128]
 
 
 def spectrum_kernel(
@@ -456,14 +461,14 @@
 
         lax.fori_loop(0, DEVICES // 8, spread, 0)
 
-        def pair_step(pair, carry, chunk=chunk):
-            column_pair(
-                pair, chunk, first_column, gather, (col_a, col_b, col_m, col_p),
+        def column_step(index, carry, chunk=chunk):
+            column_set(
+                index, chunk, first_column, gather, (col_a, col_b, col_m, col_p),
                 (col_twist, half_twist), edges, field,
             )
             return carry
 
-        lax.fori_loop(0, 8, pair_step, 0)
+        lax.fori_loop(0, 16 // COLUMNS, column_step, 0)
 
         def pack_field(i, chunk=chunk):
             device = other(i)

time: 124 us -> 120 us (0.968)
  Pallas kernels: 124 us -> 120 us
    pallas_call x1, Pallas kernels: 102 us -> 97.7 us  [exchange(): pl.pallas_call(spectrum_kernel, out_shape=(jax.ShapeDtypeStruct((2, DEVIC...]
where the time goes in v3:
time: 120 us
  Pallas kernels  120 us (100%)
    pallas_call x1, Pallas kernels, exchange(): pl.pallas_call(spectrum_kernel, out_shape=(jax.ShapeDtypeStruct((2, DEVIC...  97.7 us
    pallas_call x1, Pallas kernels, height_map(): pl.pallas_call(height_kernel, out_shape=jax.ShapeDtypeStruct((KEPT, W), b...  22.4 us

profile of v3, /device:TPU:2, one launch (start us, length us, event | category | flops | bytes accessed | tf_op | source)
XLA Modules:
  0.0 120.1 jit_solution(16295516980651590060)
XLA Ops:
  0.0 97.7 %spectrum.1 = (bf16[2,128,32,128]{3,2,1,0:T(8,128)(2,1)}, f32[128,1,128]{2,1,0:T(1,128)}) custom-call(s32[2,64]{1,0:T(2,128)} %bitcast.3, bf16[256,32768]{1,0:T(8,128)(2,1)} %fringes.1, f32[4,32]{1,0:T(4,128)} %zones.1, bf16[2,256,128]{2,1,0:T(8,128)(2,1)} %constant.22.clone.refs_0_, f32[16,2,16,8,128]{4,3,2,1,0:T(8,128)} %constant.23.clone.refs_1_, ...), custom_call_target="tpu_custom_call" | custom-call | tf_op jit(solution)/shard_map/spectrum/pallas_call | solution.py:509
  97.7 22.4 %heights.1 = bf16[128,32768]{1,0:T(8,128)(2,1)} custom-call(s32[8,64]{1,0:T(8,128)} %zone_index.1, f32[128,128]{1,0:T(8,128)} %bitcast.2, bf16[2,128,32,128]{3,2,1,0:T(8,128)(2,1)} %get-tuple-element.8.received_in, bf16[16,256,128]{2,1,0:T(8,128)(2,1)} %constant.30.clone.pix_j_in, f32[32,2,8,8,128]{4,3,2,1,0:T(8,128)} %constant.31.clone.pix_twist_in, ...), custom_call_target="tpu_custom_call" | custom-call | tf_op jit(solution)/shard_map/heights/pallas_call | solution.py:680

commit v4 on v3

--- a/solution.py
+++ b/solution.py
@@ -53,7 +53,7 @@
     cosine, sine = turns(n16, n16, 16)
     half["row_a"] = np.kron(np.concatenate([cosine[:9], -sine[1:8]], 0), np.eye(16))
     cosine, sine = turns(n16, n2048, W)
-    full["row_twist"] = by_tile(np.stack([cosine, sine], 1))
+    full["row_twist"] = np.stack([cosine, sine], 1).reshape(512, 128)
     sides = []
     for odd in range(2):
         cosine, sine = turns(n1024, LOBE_START // 16 + 2 * n128 + odd, 2048)
@@ -129,7 +129,7 @@
             return mixed[index * 16 : (index + 1) * 16, upper * 128 : (upper + 1) * 128]
 
         def factor(k, index, upper):
-            value = twist[k, index, upper * 8 + tile]
+            value = twist[(k * 2 + index) * 16 + upper * 8 + tile]
             return jnp.concatenate([value, value], axis=0)
 
         for k in range(16):
@@ -247,8 +247,8 @@
     out, zones_out, *refs = refs
     tables, refs = refs[:9], refs[9:]
     row_a, row_twist, row_b, col_a, col_b, col_m, col_p, col_twist, half_twist = tables
-    block, mid, lobe, send_a, recv_a, gather, field, send_c, edges, zone_rows, zone_row = refs[:11]
-    load_sem, send_sem, recv_sem, own_sem, table_sem = refs[11:]
+    block, mid, lobe, send_a, recv_a, gather, field, send_c, edges, zone_rows, zone_row, twists = refs[:12]
+    load_sem, send_sem, recv_sem, own_sem, table_sem = refs[12:]
     table_copies = [
         pltpu.make_async_copy(given[i], tables[i], table_sem.at[i]) for i in range(9)
     ]
@@ -265,8 +265,12 @@
 
     barrier = pltpu.get_barrier_semaphore()
 
-    def greet(i, carry):
+    def greet(i):
         pl.semaphore_signal(barrier, inc=1, device_id=place(other(i)), device_id_type=MESH)
+
+    def greet_step(i, carry):
+        for u in range(8):
+            greet(i * 8 + u)
         return carry
 
     def load(group, slot):
@@ -293,28 +297,21 @@
         pltpu.make_async_copy(others, others, send_sem.at[index]).wait()
 
     load(0, 0).start()
-    for copy in table_copies:
+    for copy in table_copies[:3]:
         copy.start()
-    lax.fori_loop(1, DEVICES, greet, 0)
-
-    lanes = lax.broadcasted_iota(jnp.int32, (1, 256), 1)
-
-    def edge_step(t, carry):
-        mine = (lanes >= 4 * t) & (lanes < 4 * t + 4)
-        return tuple(jnp.where(mine, bounds[side, t], carry[side]) for side in range(2))
-
-    both = lax.fori_loop(0, 64, edge_step, (jnp.zeros((1, 256), jnp.int32),) * 2)
-    edges[0] = both[0]
-    edges[1] = both[1]
-    zone_rows[...] = jnp.zeros((8, 128), f32)
-    zone_rows[0:4, 0:32] = zones[...]
-    spread_rows = zone_rows[...]
-    zone_row[...] = spread_rows[0:1] + sum(
-        pltpu.roll(spread_rows, 32 * r, 1)[r : r + 1] for r in range(1, 4)
-    )
+    for i in range(1, 8):
+        greet(i)
+    lax.fori_loop(1, DEVICES // 8, greet_step, 0)
 
     table_copies[0].wait()
     table_copies[1].wait()
+
+    def fill(i, carry):
+        for u in range(8):
+            twists[i * 8 + u] = jnp.broadcast_to(row_twist[pl.ds(i * 8 + u, 1), :], (8, 128))
+        return carry
+
+    lax.fori_loop(0, 64, fill, 0)
 
     def first_only(group):
         slot = lax.rem(group, 2)
@@ -323,7 +320,7 @@
 
         def piece(pair, carry):
             for rows16 in range(2):
-                row_first(block.at[slot], pair, rows16, row_a, row_twist, mid.at[slot])
+                row_first(block.at[slot], pair, rows16, row_a, twists, mid.at[slot])
             return carry
 
         lax.fori_loop(0, 4, piece, 0)
@@ -339,7 +336,7 @@
                 mid.at[1 - slot], lax.div(i, 2), lax.rem(i, 2), row_b, lobe, lax.rem(group - 1, 4)
             )
             for rows16 in range(2):
-                row_first(block.at[slot], i, rows16, row_a, row_twist, mid.at[slot])
+                row_first(block.at[slot], i, rows16, row_a, twists, mid.at[slot])
             return carry
 
         lax.fori_loop(0, 4, piece, 0)
@@ -394,7 +391,15 @@
         return carry
 
     lax.fori_loop(0, 2, quarter_step, 0)
-
+    for copy in table_copies[3:]:
+        copy.start()
+
+    zone_rows[...] = jnp.zeros((8, 128), f32)
+    zone_rows[0:4, 0:32] = zones[...]
+    spread_rows = zone_rows[...]
+    zone_row[...] = spread_rows[0:1] + sum(
+        pltpu.roll(spread_rows, 32 * r, 1)[r : r + 1] for r in range(1, 4)
+    )
     keep(zone_row, zones_out.at[me], 4)
 
     def send_zones(i, carry):
@@ -430,12 +435,29 @@
     lax.fori_loop(1, 32, pack_half_step, 0)
     keep(send_a.at[3, me], recv_a.at[3, me], 3)
 
-    def send_last(i, carry):
+    def send_last(i):
         send(send_a.at[3, other(i)], recv_a.at[3, me], other(i), 3)
-        return carry
-
-    lax.fori_loop(1, DEVICES, send_last, 0)
+
+    for i in range(1, 4):
+        send_last(i)
+
+    def last_step(i, carry):
+        for u in range(4):
+            send_last(i * 4 + u)
+        return carry
+
+    lax.fori_loop(1, DEVICES // 4, last_step, 0)
     lax.fori_loop(1, DEVICES, send_zones, 0)
+
+    lanes = lax.broadcasted_iota(jnp.int32, (1, 256), 1)
+
+    def edge_step(t, carry):
+        mine = (lanes >= 4 * t) & (lanes < 4 * t + 4)
+        return tuple(jnp.where(mine, bounds[side, t], carry[side]) for side in range(2))
+
+    both = lax.fori_loop(0, 64, edge_step, (jnp.zeros((1, 256), jnp.int32),) * 2)
+    edges[0] = both[0]
+    edges[1] = both[1]
 
     first_column = lax.div(me, 4) + 32 * 32 * lax.rem(me, 4)
     low_lanes = lax.broadcasted_iota(jnp.int32, (32, 128), 1) < 64
@@ -532,6 +554,7 @@
             pltpu.VMEM((2, 1, 256), jnp.int32),
             pltpu.VMEM((8, 128), f32),
             pltpu.VMEM((1, 128), f32),
+            pltpu.VMEM((512, 8, 128), f32),
             pltpu.SemaphoreType.DMA((2,)),
             pltpu.SemaphoreType.DMA((7,)),
             pltpu.SemaphoreType.DMA((7,)),

time: 120 us -> 119 us (level)
  no operation moved by 1% of the time
where the time goes in v4:
time: 119 us
  Pallas kernels  119 us (100%)
    pallas_call x1, Pallas kernels, exchange(): pl.pallas_call(spectrum_kernel, out_shape=(jax.ShapeDtypeStruct((2, DEVIC...  96.5 us
    pallas_call x1, Pallas kernels, height_map(): pl.pallas_call(height_kernel, out_shape=jax.ShapeDtypeStruct((KEPT, W), b...  22.4 us

profile of v4, /device:TPU:2, one launch (start us, length us, event | category | flops | bytes accessed | tf_op | source)
XLA Modules:
  0.0 118.9 jit_solution(1538602129622521010)
XLA Ops:
  0.0 96.5 %spectrum.1 = (bf16[2,128,32,128]{3,2,1,0:T(8,128)(2,1)}, f32[128,1,128]{2,1,0:T(1,128)}) custom-call(s32[2,64]{1,0:T(2,128)} %bitcast.3, bf16[256,32768]{1,0:T(8,128)(2,1)} %fringes.1, f32[4,32]{1,0:T(4,128)} %zones.1, bf16[2,256,128]{2,1,0:T(8,128)(2,1)} %constant.22.clone.refs_0_, f32[512,128]{1,0:T(8,128)} %constant.23.clone.refs_1_, ...), custom_call_target="tpu_custom_call" | custom-call | tf_op jit(solution)/shard_map/spectrum/pallas_call | solution.py:531
  96.5 22.4 %heights.1 = bf16[128,32768]{1,0:T(8,128)(2,1)} custom-call(s32[8,64]{1,0:T(8,128)} %zone_index.1, f32[128,128]{1,0:T(8,128)} %bitcast.2, bf16[2,128,32,128]{3,2,1,0:T(8,128)(2,1)} %get-tuple-element.8.received_in, bf16[16,256,128]{2,1,0:T(8,128)(2,1)} %constant.30.clone.pix_j_in, f32[32,2,8,8,128]{4,3,2,1,0:T(8,128)} %constant.31.clone.pix_twist_in, ...), custom_call_target="tpu_custom_call" | custom-call | tf_op jit(solution)/shard_map/heights/pallas_call | solution.py:703
